TPU v7x, 512 devices: a whole 4x4x16 slice. The times are simulated.
512 devices in a mesh: cube: 64 (over z_lo, x, core), col: 8 (over z_hi, y).
Axes of the slice: x: 4, y: 4, z: 16 (z_hi: 2, z_lo: 8; z = z_hi * 8 + z_lo), core: 2. Of those that a mesh axis runs over, the one named last changes fastest.
Arguments:
- front_matrix: float32 [12288, 12288], P('cube', 'col'), may hold values from -6 to 6
- child_tiles: bfloat16 [64, 8, 128, 32, 128], P('cube', 'col'), may hold values from -6 to 6
- dest_cube: int32 [64, 8, 128, 1], P('cube', 'col'), may hold values from 0 to 63; in each aligned block of 128 rows (0 to 127, 128 to 255, ..., all dimensions but the last counted through in order) at most 4 rows name the same one
- dest_slot: int32 [64, 8, 128], P('cube', 'col'), may hold values from 0 to 71
- diag_inverse: bfloat16 [512, 512], replicated, may hold values from -0.0546875 to 0.0546875
Outputs:
- factored: float32 [12288, 12288], P('cube', 'col')
Inputs may be any that keep to these rules, and one draw needn't show every extreme that they name: `dest_cube`: among the tiles held by one device, at most 4 name the same row block, and every draw has a device where some row block is named exactly 4 times.
All inputs are finite; a program needn't handle non-finite values.
Results may differ from a plain program's by a relative error of at most 0.0043.
Values may be sent and summed in bfloat16 or wider, within the bound.
A program may use at most 64 MiB of HBM per device.

v0:
```python
import jax
import jax.numpy as jnp
from jax import lax
from jax.sharding import PartitionSpec as P

CAP = 4


def from_root(value, axis, source):
    kept = jnp.where(lax.axis_index(axis) == source, value, 0).astype(value.dtype)
    return lax.psum(kept, axis)


def local(front_matrix, child_tiles, dest_cube, dest_slot, diag_inverse):
    cube_count = lax.axis_size("cube")
    col_index = lax.axis_index("col")
    rows_local, cols_local = front_matrix.shape
    tile_count = child_tiles.shape[2]
    tile_rows = child_tiles.shape[3]
    tile_width = child_tiles.shape[4]
    capacity = CAP
    tile_cols = cols_local // tile_width
    slots_local = rows_local // tile_rows * tile_cols
    flat_tiles = child_tiles.reshape(tile_count, tile_rows * tile_width)
    target = dest_cube.reshape(tile_count)
    slot_ids = dest_slot.reshape(tile_count)
    onehot = (target[:, None] == jnp.arange(cube_count, dtype=jnp.int32)[None, :]).astype(jnp.int32)
    before = jnp.cumsum(onehot, axis=0) - onehot
    position = jnp.sum(before * onehot, axis=1)
    buffer_row = target * capacity + position
    send_tiles = (
        jnp.zeros((cube_count * capacity, tile_rows * tile_width), jnp.bfloat16)
        .at[buffer_row]
        .set(flat_tiles)
    )
    send_slots = (
        jnp.full((cube_count * capacity,), slots_local, jnp.int32).at[buffer_row].set(slot_ids)
    )
    got_tiles, got_slots = (
        lax.all_to_all(
            send_tiles.reshape(cube_count, capacity, tile_rows * tile_width),
            "cube",
            split_axis=0,
            concat_axis=0,
            tiled=True,
        ),
        lax.all_to_all(
            send_slots.reshape(cube_count, capacity),
            "cube",
            split_axis=0,
            concat_axis=0,
            tiled=True,
        ),
    )
    got_tiles = got_tiles.reshape(cube_count * capacity, tile_rows * tile_width)
    got_slots = got_slots.reshape(cube_count * capacity)
    select = (jnp.arange(slots_local, dtype=jnp.int32)[:, None] == got_slots[None, :]).astype(
        jnp.bfloat16
    )
    extend_sum = jnp.dot(select, got_tiles, preferred_element_type=jnp.float32)
    extend_sum = (
        extend_sum.reshape(rows_local // tile_rows, tile_cols, tile_rows, tile_width)
        .transpose(0, 2, 1, 3)
        .reshape(rows_local, cols_local)
    )
    assembled = front_matrix + extend_sum
    panel_width = diag_inverse.shape[0]

    def make_panel(values):
        return jnp.dot(
            values[:, :panel_width].astype(jnp.bfloat16),
            diag_inverse,
            preferred_element_type=jnp.float32,
        ).astype(jnp.bfloat16)

    def empty_panel(values):
        return jnp.zeros((rows_local, panel_width), jnp.bfloat16)

    panel_own = lax.cond(col_index == 0, make_panel, empty_panel, assembled)
    panel_factor = from_root(panel_own, "col", 0)
    all_panel = lax.all_gather(panel_factor, "cube", axis=0, tiled=True)
    across = lax.dynamic_slice_in_dim(all_panel, col_index * cols_local, cols_local, 0)
    update = lax.dot_general(
        panel_factor, across, (((1,), (1,)), ((), ())), preferred_element_type=jnp.float32
    )
    trailing = assembled - update
    global_col = col_index * cols_local + jnp.arange(cols_local, dtype=jnp.int32)
    panel_wide = jnp.pad(panel_factor.astype(jnp.float32), ((0, 0), (0, cols_local - panel_width)))
    return jnp.where(global_col[None, :] < panel_width, panel_wide, trailing)


def solution(mesh):
    in_specs = (
        P("cube", "col"),
        P("cube", "col", None, None, None),
        P("cube", "col", None, None),
        P("cube", "col", None),
        P(),
    )
    out_specs = P("cube", "col")
    return jax.shard_map(local, mesh=mesh, in_specs=in_specs, out_specs=out_specs, check_vma=False)
```

profile of v0, /device:TPU:1, one launch (start us, length us, event | category | flops | bytes accessed | tf_op | source)
XLA Modules:
  0.0 436.4 jit_solution(90561424863732299)
XLA Ops:
  6.5 0.7 fusion.9
  7.3 0.2 reduce_window_sum.11
  7.4 0.8 select_reduce_fusion
  8.3 0.7 fusion.12
  8.9 1.1 scatter_custom_fusion
  10.1 0.7 all_to_all.9
  10.8 17.0 %all-to-all-start = ((s32[64,1,4]{2,1,0:T(1,128)}), s32[64,1,4]{2,1,0:T(1,128)S(1)}, u32[]{:S(2)}, u32[]{:S(2)}) async-start(s32[64,1,4]{2,1,0:T(1,128)} %bitcast.5), calls=%async_computation | async-start | bytes 65536 | tf_op jit(solution)/shard_map/all_to_all | solution.py:47
  27.8 3.6 scatter_custom_fusion.1
  31.5 2.2 reshape.79
  33.7 6.3 %all-to-all-done = s32[64,1,4]{2,1,0:T(1,128)S(1)} async-done(((s32[64,1,4]{2,1,0:T(1,128)}), s32[64,1,4]{2,1,0:T(1,128)S(1)}, u32[]{:S(2)}, u32[]{:S(2)}) %all-to-all-start) | async-done | bytes 1056 | tf_op jit(solution)/shard_map/all_to_all | solution.py:47
  40.0 6.8 %all-to-all-start.1 = ((bf16[64,4,4096]{2,1,0:T(4,128)(2,1)}), bf16[64,4,4096]{2,1,0:T(4,128)(2,1)S(1)}, u32[]{:S(2)}, u32[]{:S(2)}) async-start(bf16[64,4,4096]{2,1,0:T(4,128)(2,1)} %reshape.79), calls=%async_computation.1 | async-start | bytes 4194304 | tf_op jit(solution)/shard_map/all_to_all | solution.py:40
  46.9 0.0 all-reduce.3.cloned.1.call-start
  46.9 0.5 broadcast.73
  47.4 0.7 reduce.3
  48.2 0.1 eq.54
  48.3 94.2 %all-to-all-done.1 = bf16[64,4,4096]{2,1,0:T(4,128)(2,1)S(1)} async-done(((bf16[64,4,4096]{2,1,0:T(4,128)(2,1)}), bf16[64,4,4096]{2,1,0:T(4,128)(2,1)S(1)}, u32[]{:S(2)}, u32[]{:S(2)}) %all-to-all-start.1) | async-done | bytes 2097184 | tf_op jit(solution)/shard_map/all_to_all | solution.py:40
  142.5 2.1 reshape.80
  144.5 3.3 copy.9
  147.8 0.0 copy-start
  147.8 0.8 fusion.6
  148.6 0.5 copy-done
  149.1 0.0 copy-start.1
  149.1 0.6 bitcast_add_fusion
  149.6 0.5 copy-done.1
  150.1 0.3 conditional.1
  150.1 0.3 convolution_convert_fusion
  150.4 0.7 broadcast_select_fusion
  151.1 0.0 all-reduce.3.cloned.1.call-update
  151.1 0.0 all-gather.2.cloned.1.call-start
  151.2 142.9 %all-reduce.3.cloned.1.call-done = bf16[192,512]{1,0:T(8,128)(2,1)} async-done(((bf16[192,512]{1,0:T(8,128)(2,1)}), bf16[192,512]{1,0:T(8,128)(2,1)}) %all-reduce.3.cloned.1.call-update) | async-done | bytes 196624 | tf_op jit(solution)/shard_map/psum | solution.py:11
  294.0 0.0 all-gather.2.cloned.1.call-update
  294.1 132.3 %all-gather.2.cloned.1.call-done = bf16[12288,512]{1,0:T(8,128)(2,1)} async-done(((bf16[192,512]{1,0:T(8,128)(2,1)}), bf16[12288,512]{1,0:T(8,128)(2,1)}) %all-gather.2.cloned.1.call-update) | async-done | bytes 12582928 | tf_op jit(solution)/shard_map/all_gather | solution.py:81
  426.4 3.1 fusion
  (2 shorter events, 0.0 us)
Async XLA Ops:
  10.8 29.3 %all-to-all-start = ((s32[64,1,4]{2,1,0:T(1,128)}), s32[64,1,4]{2,1,0:T(1,128)S(1)}, u32[]{:S(2)}, u32[]{:S(2)}) async-start(s32[64,1,4]{2,1,0:T(1,128)} %bitcast.5), calls=%async_computation | async-start | bytes 65536 | tf_op jit(solution)/shard_map/all_to_all | solution.py:47
  40.0 102.4 %all-to-all-start.1 = ((bf16[64,4,4096]{2,1,0:T(4,128)(2,1)}), bf16[64,4,4096]{2,1,0:T(4,128)(2,1)S(1)}, u32[]{:S(2)}, u32[]{:S(2)}) async-start(bf16[64,4,4096]{2,1,0:T(4,128)(2,1)} %reshape.79), calls=%async_computation.1 | async-start | bytes 4194304 | tf_op jit(solution)/shard_map/all_to_all | solution.py:40
  46.9 247.2 %all-reduce.3.cloned.1.call-start = ((), (), s32[]{:S(2)}) async-start(), calls=%async_computation.2 | async-start | bytes 393216 | tf_op jit(solution)/shard_map/psum | solution.py:11
  147.8 1.3 copy-start
  149.1 1.0 copy-start.1
  151.1 275.3 %all-gather.2.cloned.1.call-start = ((), (), s32[]{:S(2)}) async-start(), calls=%async_computation.3 | async-start | bytes 12779520 | tf_op jit(solution)/shard_map/all_gather | solution.py:81
Sparse Core Ops, SparseCore 0:
  151.2 142.7 all-reduce.2
  296.4 129.9 all-gather.1
where the time goes:
time: 437 us; the launch traced here: 436 us
  waiting for transfers between devices  376 us (86%)
  starting transfers between devices  23.9 us (5%)
  local copies, waits for them, and re-layouts  14.6 us (3%)
  between operations  13.5 us (3%)
  other arithmetic  4.4 us (1%)
    psum x1, waiting for transfers between devices, from_root(): return lax.psum(kept, axis)  143 us
    all_gather x1, waiting for transfers between devices, local(): all_panel = lax.all_gather(panel_factor, 'cube', axis=0, tiled=True)  132 us
    all_to_all x1, waiting for transfers between devices, local(): lax.all_to_all(send_tiles.reshape(cube_count, capacity, tile_rows * tile_...  94.2 us
    all_to_all x1, starting transfers between devices, local(): lax.all_to_all(send_slots.reshape(cube_count, capacity), 'cube', split_ax...  17 us
  transfers between devices with their start and end apart: 4, of which 4 were waited for; matrix products, arithmetic and copies ran while one was open for 2% of the time, Pallas kernels for 0%

commit v1 on v0

--- a/solution.py
+++ b/solution.py
@@ -1,19 +1,243 @@
+import functools
+
 import jax
 import jax.numpy as jnp
 from jax import lax
+from jax.experimental import pallas as pl
+from jax.experimental.pallas import tpu as pltpu
 from jax.sharding import PartitionSpec as P
 
 CAP = 4
-
-
-def from_root(value, axis, source):
-    kept = jnp.where(lax.axis_index(axis) == source, value, 0).astype(value.dtype)
-    return lax.psum(kept, axis)
+MESH = pl.DeviceIdType.MESH
+QUARTERS = 4
+MIDDLE = 4
+BLOCKS = 8
+
+
+def spread_kernel(
+    assembled_ref,
+    diag_ref,
+    out_ref,
+    own,
+    across,
+    own_recv,
+    across_recv,
+    down_send,
+    cross_send,
+    level_send,
+    entry_send,
+    chain_send,
+    row_send,
+    core_send,
+):
+    cube = lax.axis_index("cube")
+    col = lax.axis_index("col")
+    z = cube // 8
+    x = (cube // 2) % 4
+    core = cube % 2
+    half = col // 4
+    y = col % 4
+    block = cube % 8
+    rows, cols = assembled_ref.shape
+    width = diag_ref.shape[0]
+    depth = rows // QUARTERS
+
+    def at(z_to, x_to, core_to, half_to, y_to):
+        return {"cube": z_to * 8 + x_to * 2 + core_to, "col": half_to * 4 + y_to}
+
+    is_root = col == 0
+    is_entry = (half == 0) & (y == z % 4)
+    is_middle = z == MIDDLE
+    has_above = z < 7
+    has_below = z > 0
+    level_peers = [at(z, x, core, half, (y + s) % 4) for s in (1, 2, 3)]
+    half_peer = at(z, x, core, 1 - half, y)
+    row_peers = [at(z, (x + s) % 4, core, half, y) for s in (1, 2, 3)]
+    core_peer = at(z, x, 1 - core, half, y)
+    above = at(z + 1, x, core, half, y)
+    below = at(z - 1, x, core, half, y)
+    entry_to = at(MIDDLE, x, core, z // 4, y)
+    entry_from = at(half * 4 + y, x, core, 0, y)
+
+    barrier = pltpu.get_barrier_semaphore()
+
+    def greet(device):
+        pl.semaphore_signal(barrier, inc=1, device_id=device, device_id_type=MESH)
+
+    for device in level_peers + [half_peer] + row_peers + [core_peer]:
+        greet(device)
+    for there, device in (
+        (has_above, above),
+        (has_below, below),
+        (is_entry, entry_to),
+        (is_middle, entry_from),
+    ):
+        pl.when(there)(functools.partial(greet, device))
+
+    @pl.when(is_root)
+    def _():
+        panel = jnp.dot(
+            assembled_ref[:, :width].astype(jnp.bfloat16),
+            diag_ref[...],
+            preferred_element_type=jnp.float32,
+        ).astype(jnp.bfloat16)
+        for q in range(QUARTERS):
+            own[q] = panel[q * depth : (q + 1) * depth]
+
+    pl.semaphore_wait(
+        barrier,
+        8
+        + has_above.astype(jnp.int32)
+        + has_below.astype(jnp.int32)
+        + is_entry.astype(jnp.int32)
+        + is_middle.astype(jnp.int32),
+    )
+
+    started = []
+
+    def send(there, source, target, send_sem, recv_sem, device):
+        copy = pltpu.make_async_remote_copy(
+            src_ref=source,
+            dst_ref=target,
+            send_sem=send_sem,
+            recv_sem=recv_sem,
+            device_id=device,
+            device_id_type=MESH,
+        )
+        if there is None:
+            copy.start()
+        else:
+            pl.when(there)(copy.start)
+        started.append((there, copy))
+
+    def arrived(target, recv_sem):
+        pltpu.make_async_remote_copy(
+            src_ref=target,
+            dst_ref=target,
+            send_sem=recv_sem,
+            recv_sem=recv_sem,
+            device_id=core_peer,
+            device_id_type=MESH,
+        ).wait_recv()
+
+    first = jnp.maximum(z % 4 - 1, 0)
+    for s in range(3):
+        y_to = 1 + (first + s) % 3
+        for q in range(QUARTERS):
+            send(
+                is_root,
+                own.at[q],
+                own.at[q],
+                down_send.at[s * QUARTERS + q],
+                own_recv.at[q],
+                at(z, x, core, 0, y_to),
+            )
+
+    for q in range(QUARTERS):
+        pl.when((half == 0) & (y != 0))(functools.partial(arrived, own.at[q], own_recv.at[q]))
+        send(
+            is_entry,
+            own.at[q],
+            across.at[block, q],
+            entry_send.at[q],
+            across_recv.at[block, q],
+            entry_to,
+        )
+    send(half == 0, own.at[y], own.at[y], cross_send.at[0], own_recv.at[y], half_peer)
+
+    for q in range(QUARTERS):
+        arrived(across.at[block, q], across_recv.at[block, q])
+        mine = (across.at[block, q], across.at[block, q])
+        ready = across_recv.at[block, q]
+        send(has_above & (z >= MIDDLE), *mine, chain_send.at[q, 0], ready, above)
+        send(has_below & (z <= MIDDLE), *mine, chain_send.at[q, 1], ready, below)
+        for s in range(3):
+            send(None, *mine, row_send.at[q, s], ready, row_peers[s])
+        send(None, *mine, core_send.at[q, 0], ready, core_peer)
+        if q == 1:
+            pl.when(half == 1)(functools.partial(arrived, own.at[y], own_recv.at[y]))
+            for s in range(3):
+                send(
+                    half == 1,
+                    own.at[y],
+                    own.at[y],
+                    level_send.at[s],
+                    own_recv.at[y],
+                    level_peers[s],
+                )
+        for s in range(3):
+            theirs = ((x + s + 1) % 4) * 2 + core
+            arrived(across.at[theirs, q], across_recv.at[theirs, q])
+            send(
+                None,
+                across.at[theirs, q],
+                across.at[theirs, q],
+                core_send.at[q, s + 1],
+                across_recv.at[theirs, q],
+                core_peer,
+            )
+
+    for s in range(1, QUARTERS):
+        q = (y + s) % 4
+        pl.when(half == 1)(functools.partial(arrived, own.at[q], own_recv.at[q]))
+    for q in range(QUARTERS):
+        for s in range(4):
+            theirs = s * 2 + 1 - core
+            arrived(across.at[theirs, q], across_recv.at[theirs, q])
+
+    panel = own[...].reshape(rows, width)
+    span = cols // 4
+    for s in range(4):
+        part = across[2 * s : 2 * s + 2].reshape(span, width)
+        update = lax.dot_general(
+            panel, part, (((1,), (1,)), ((), ())), preferred_element_type=jnp.float32
+        )
+        here = slice(s * span, (s + 1) * span)
+        out_ref[:, here] = assembled_ref[:, here] - update
+
+    @pl.when(is_root)
+    def _():
+        out_ref[:, :width] = panel.astype(jnp.float32)
+
+    for there, copy in started:
+        if there is None:
+            copy.wait_send()
+        else:
+            pl.when(there)(copy.wait_send)
+
+
+def spread(assembled, diag_inverse):
+    rows, cols = assembled.shape
+    width = diag_inverse.shape[0]
+    depth = rows // QUARTERS
+    vmem = pl.BlockSpec(memory_space=pltpu.VMEM)
+    dma = pltpu.SemaphoreType.DMA
+    return pl.pallas_call(
+        spread_kernel,
+        out_shape=jax.ShapeDtypeStruct((rows, cols), jnp.float32),
+        in_specs=[vmem, vmem],
+        out_specs=vmem,
+        scratch_shapes=[
+            pltpu.VMEM((QUARTERS, depth, width), jnp.bfloat16),
+            pltpu.VMEM((BLOCKS, QUARTERS, depth, width), jnp.bfloat16),
+            dma((QUARTERS,)),
+            dma((BLOCKS, QUARTERS)),
+            dma((3 * QUARTERS,)),
+            dma((1,)),
+            dma((3,)),
+            dma((QUARTERS,)),
+            dma((QUARTERS, 2)),
+            dma((QUARTERS, 3)),
+            dma((QUARTERS, 4)),
+        ],
+        compiler_params=pltpu.CompilerParams(
+            collective_id=1, has_side_effects=True, vmem_limit_bytes=40 * 2**20
+        ),
+    )(assembled, diag_inverse)
 
 
 def local(front_matrix, child_tiles, dest_cube, dest_slot, diag_inverse):
     cube_count = lax.axis_size("cube")
-    col_index = lax.axis_index("col")
     rows_local, cols_local = front_matrix.shape
     tile_count = child_tiles.shape[2]
     tile_rows = child_tiles.shape[3]
@@ -63,30 +287,7 @@
         .transpose(0, 2, 1, 3)
         .reshape(rows_local, cols_local)
     )
-    assembled = front_matrix + extend_sum
-    panel_width = diag_inverse.shape[0]
-
-    def make_panel(values):
-        return jnp.dot(
-            values[:, :panel_width].astype(jnp.bfloat16),
-            diag_inverse,
-            preferred_element_type=jnp.float32,
-        ).astype(jnp.bfloat16)
-
-    def empty_panel(values):
-        return jnp.zeros((rows_local, panel_width), jnp.bfloat16)
-
-    panel_own = lax.cond(col_index == 0, make_panel, empty_panel, assembled)
-    panel_factor = from_root(panel_own, "col", 0)
-    all_panel = lax.all_gather(panel_factor, "cube", axis=0, tiled=True)
-    across = lax.dynamic_slice_in_dim(all_panel, col_index * cols_local, cols_local, 0)
-    update = lax.dot_general(
-        panel_factor, across, (((1,), (1,)), ((), ())), preferred_element_type=jnp.float32
-    )
-    trailing = assembled - update
-    global_col = col_index * cols_local + jnp.arange(cols_local, dtype=jnp.int32)
-    panel_wide = jnp.pad(panel_factor.astype(jnp.float32), ((0, 0), (0, cols_local - panel_width)))
-    return jnp.where(global_col[None, :] < panel_width, panel_wide, trailing)
+    return spread(front_matrix + extend_sum, diag_inverse)
 
 
 def solution(mesh):

time: 437 us -> 195 us (0.45)
  waiting for transfers between devices: 376 us -> 101 us
  Pallas kernels: 0 us -> 48.5 us
  between operations: 13.5 us -> 0.1 us
    psum x1 -> x0, waiting for transfers between devices: 143 us -> none  [from_root(): return lax.psum(kept, axis)]
    all_gather x1 -> x0, waiting for transfers between devices: 132 us -> none  [local(): all_panel = lax.all_gather(panel_factor, 'cube', axis=0, tiled=True)]
    pallas_call x0 -> x1, Pallas kernels: none -> 48.5 us  [spread(): pl.pallas_call(spread_kernel, out_shape=jax.ShapeDtypeStruct((rows, cols)...]
  transfers between devices with their start and end apart: 4 -> 2, of which waited for: 4 -> 2; matrix products, arithmetic and copies ran while one was open for 2% -> 4% of each run, Pallas kernels for 0% -> 0%
where the time goes in v1:
time: 195 us; the launch traced here: 193 us
  waiting for transfers between devices  101 us (52%)
  Pallas kernels  48.5 us (25%)
  starting transfers between devices  23.9 us (12%)
  local copies, waits for them, and re-layouts  15.2 us (8%)
  other arithmetic  3.7 us (2%)
    all_to_all x1, waiting for transfers between devices, local(): lax.all_to_all(send_tiles.reshape(cube_count, capacity, tile_rows * tile_...  94.2 us
    pallas_call x1, Pallas kernels, spread(): pl.pallas_call(spread_kernel, out_shape=jax.ShapeDtypeStruct((rows, cols)...  48.5 us
    all_to_all x1, starting transfers between devices, local(): lax.all_to_all(send_slots.reshape(cube_count, capacity), 'cube', split_ax...  17 us
    all_to_all x1, starting transfers between devices, local(): lax.all_to_all(send_tiles.reshape(cube_count, capacity, tile_rows * tile_...  6.82 us
    all_to_all x1, waiting for transfers between devices, local(): lax.all_to_all(send_slots.reshape(cube_count, capacity), 'cube', split_ax...  6.34 us
  transfers between devices with their start and end apart: 2, of which 2 were waited for; matrix products, arithmetic and copies ran while one was open for 4% of the time, Pallas kernels for 0%

profile of v1, /device:TPU:1, one launch (start us, length us, event | category | flops | bytes accessed | tf_op | source)
XLA Modules:
  0.0 192.7 jit_solution(14607015013534442922)
XLA Ops:
  0.0 0.7 fusion.7
  0.7 0.2 reduce_window_sum.11
  0.9 0.8 select_reduce_fusion
  1.7 0.7 fusion.10
  2.4 1.1 scatter_custom_fusion
  3.5 0.7 all_to_all.9
  4.2 17.0 %all-to-all-start = ((s32[64,1,4]{2,1,0:T(1,128)}), s32[64,1,4]{2,1,0:T(1,128)S(1)}, u32[]{:S(2)}, u32[]{:S(2)}) async-start(s32[64,1,4]{2,1,0:T(1,128)} %bitcast.5), calls=%async_computation | async-start | bytes 65536 | tf_op jit(solution)/shard_map/all_to_all | solution.py:271
  21.3 3.6 %scatter_custom_fusion.1 = bf16[256,4096]{1,0:T(8,128)(2,1)S(1)} fusion(s32[128]{0:T(128)S(1)} %fusion.10, bf16[16,8,32,128]{3,2,1,0:T(8,128)(2,1)} %bitcast.34, bf16[]{:T(256)} %constant.16.clone.1), kind=kCustom, calls=%fused_computation.3 | custom fusion | bytes 3145730 | tf_op jit(solution)/shard_map/scatter | solution.py:258
  24.9 2.2 %reshape.73 = bf16[64,4,4096]{2,1,0:T(4,128)(2,1)} reshape(bf16[256,4096]{1,0:T(8,128)(2,1)S(1)} %scatter_custom_fusion.1) | data formatting | bytes 4194304 | tf_op jit(solution)/shard_map/reshape | solution.py:265
  27.2 6.3 %all-to-all-done = s32[64,1,4]{2,1,0:T(1,128)S(1)} async-done(((s32[64,1,4]{2,1,0:T(1,128)}), s32[64,1,4]{2,1,0:T(1,128)S(1)}, u32[]{:S(2)}, u32[]{:S(2)}) %all-to-all-start) | async-done | bytes 1056 | tf_op jit(solution)/shard_map/all_to_all | solution.py:271
  33.5 6.8 %all-to-all-start.1 = ((bf16[64,4,4096]{2,1,0:T(4,128)(2,1)}), bf16[64,4,4096]{2,1,0:T(4,128)(2,1)S(1)}, u32[]{:S(2)}, u32[]{:S(2)}) async-start(bf16[64,4,4096]{2,1,0:T(4,128)(2,1)} %reshape.73), calls=%async_computation.1 | async-start | bytes 4194304 | tf_op jit(solution)/shard_map/all_to_all | solution.py:264
  40.3 0.5 broadcast.59
  40.9 0.7 reduce.3
  41.6 0.1 eq.49
  41.7 94.2 %all-to-all-done.1 = bf16[64,4,4096]{2,1,0:T(4,128)(2,1)S(1)} async-done(((bf16[64,4,4096]{2,1,0:T(4,128)(2,1)}), bf16[64,4,4096]{2,1,0:T(4,128)(2,1)S(1)}, u32[]{:S(2)}, u32[]{:S(2)}) %all-to-all-start.1) | async-done | bytes 2097184 | tf_op jit(solution)/shard_map/all_to_all | solution.py:264
  135.9 2.1 %reshape.74 = bf16[256,4096]{1,0:T(8,128)(2,1)} reshape(bf16[64,4,4096]{2,1,0:T(4,128)(2,1)S(1)} %all-to-all-done.1) | data formatting | bytes 4194304 | tf_op jit(solution)/shard_map/reshape | solution.py:279
  138.0 3.3 %copy.8 = bf16[4096,256]{1,0:T(8,128)(2,1)S(1)} copy(bf16[4096,256]{0,1:T(8,128)(2,1)} %bitcast.32) | data formatting | bytes 4194304 | tf_op jit(solution)/shard_map/dot_general | solution.py:284
  141.3 0.0 copy-start.1
  141.3 0.8 fusion.4
  142.0 0.0 copy-start
  142.1 0.5 copy-done.1
  142.5 0.6 bitcast_add_fusion.assembled_ref
  143.1 0.1 copy-done
  143.2 48.5 %shard_map.55 = f32[192,1536]{1,0:T(8,128)S(1)} custom-call(f32[192,1536]{1,0:T(8,128)S(1)} %bitcast_add_fusion.assembled_ref, bf16[512,512]{1,0:T(8,128)(2,1)S(1)} %copy-done), custom_call_target="tpu_custom_call" | custom-call | tf_op jit(solution)/shard_map/pallas_call | solution.py:215
  191.7 1.0 copy.18
  (1 shorter events, 0.0 us)
Async XLA Ops:
  4.2 29.3 %all-to-all-start = ((s32[64,1,4]{2,1,0:T(1,128)}), s32[64,1,4]{2,1,0:T(1,128)S(1)}, u32[]{:S(2)}, u32[]{:S(2)}) async-start(s32[64,1,4]{2,1,0:T(1,128)} %bitcast.5), calls=%async_computation | async-start | bytes 65536 | tf_op jit(solution)/shard_map/all_to_all | solution.py:271
  33.5 102.4 %all-to-all-start.1 = ((bf16[64,4,4096]{2,1,0:T(4,128)(2,1)}), bf16[64,4,4096]{2,1,0:T(4,128)(2,1)S(1)}, u32[]{:S(2)}, u32[]{:S(2)}) async-start(bf16[64,4,4096]{2,1,0:T(4,128)(2,1)} %reshape.73), calls=%async_computation.1 | async-start | bytes 4194304 | tf_op jit(solution)/shard_map/all_to_all | solution.py:264
  141.3 1.3 copy-start.1
  142.0 1.1 copy-start

commit v2 on v1

--- a/solution.py
+++ b/solution.py
@@ -8,6 +8,7 @@
 from jax.sharding import PartitionSpec as P
 
 CAP = 4
+EMPTY = 72
 MESH = pl.DeviceIdType.MESH
 QUARTERS = 4
 MIDDLE = 4
@@ -236,58 +237,173 @@
     )(assembled, diag_inverse)
 
 
+def pack_kernel(cube_ref, slot_ref, tiles_ref, send_ref, slots_ref, counts):
+    groups = send_ref.shape[0]
+    slots_ref[...] = jnp.full(slots_ref.shape, EMPTY, jnp.int32)
+    lane = lax.broadcasted_iota(jnp.int32, (1, slots_ref.shape[2]), 1)
+
+    def clear(g, carry):
+        counts[g] = 0
+        return carry
+
+    lax.fori_loop(0, groups, clear, 0, unroll=8)
+
+    def place(t, carry):
+        g = cube_ref[t]
+        p = counts[g]
+        counts[g] = p + 1
+        send_ref[g, p] = tiles_ref[t]
+        slots_ref[g] = jnp.where(lane == p, slot_ref[t], slots_ref[g])
+        return carry
+
+    lax.fori_loop(0, tiles_ref.shape[0], place, 0, unroll=4)
+
+
+def pack(target, slot_ids, tiles, groups):
+    smem = pl.BlockSpec(memory_space=pltpu.SMEM)
+    vmem = pl.BlockSpec(memory_space=pltpu.VMEM)
+    return pl.pallas_call(
+        pack_kernel,
+        out_shape=(
+            jax.ShapeDtypeStruct((groups, CAP) + tiles.shape[1:], tiles.dtype),
+            jax.ShapeDtypeStruct((groups, 1, 128), jnp.int32),
+        ),
+        in_specs=[smem, smem, vmem],
+        out_specs=(vmem, vmem),
+        scratch_shapes=[pltpu.SMEM((groups,), jnp.int32)],
+        compiler_params=pltpu.CompilerParams(vmem_limit_bytes=40 * 2**20),
+    )(target, slot_ids, tiles)
+
+
+def exchange_kernel(
+    send_ref, slots_ref, got_ref, got_slots_ref, tile_send, tile_recv, slot_send, slot_recv, self_sem
+):
+    groups = send_ref.shape[0]
+    me = lax.axis_index("cube")
+    barrier = pltpu.get_barrier_semaphore()
+
+    def partner(step):
+        return me ^ ((step % 8) * 8 + step // 8)
+
+    def greet(step, carry):
+        pl.semaphore_signal(
+            barrier, inc=1, device_id={"cube": partner(step)}, device_id_type=MESH
+        )
+        return carry
+
+    lax.fori_loop(1, groups, greet, 0)
+    kept = pltpu.make_async_copy(send_ref.at[me], got_ref.at[me], self_sem.at[0])
+    kept_slots = pltpu.make_async_copy(slots_ref.at[me], got_slots_ref.at[me], self_sem.at[1])
+    kept.start()
+    kept_slots.start()
+    pl.semaphore_wait(barrier, groups - 1)
+
+    def copies(step):
+        to = partner(step)
+        return (
+            pltpu.make_async_remote_copy(
+                src_ref=slots_ref.at[to],
+                dst_ref=got_slots_ref.at[me],
+                send_sem=slot_send.at[step],
+                recv_sem=slot_recv.at[step],
+                device_id={"cube": to},
+                device_id_type=MESH,
+            ),
+            pltpu.make_async_remote_copy(
+                src_ref=send_ref.at[to],
+                dst_ref=got_ref.at[me],
+                send_sem=tile_send.at[step],
+                recv_sem=tile_recv.at[step],
+                device_id={"cube": to},
+                device_id_type=MESH,
+            ),
+        )
+
+    def start(step, carry):
+        for copy in copies(step):
+            copy.start()
+        return carry
+
+    lax.fori_loop(1, groups, start, 0)
+
+    def finish(step, carry):
+        for copy in copies(step):
+            copy.wait()
+        return carry
+
+    lax.fori_loop(1, groups, finish, 0)
+    kept.wait()
+    kept_slots.wait()
+
+
+def exchange(send_tiles, send_slots):
+    groups = send_tiles.shape[0]
+    anywhere = pl.BlockSpec(memory_space=pl.ANY)
+    dma = pltpu.SemaphoreType.DMA
+    return pl.pallas_call(
+        exchange_kernel,
+        out_shape=(
+            jax.ShapeDtypeStruct(send_tiles.shape, send_tiles.dtype),
+            jax.ShapeDtypeStruct(send_slots.shape, send_slots.dtype),
+        ),
+        in_specs=[anywhere, anywhere],
+        out_specs=(anywhere, anywhere),
+        scratch_shapes=[
+            dma((groups,)),
+            dma((groups,)),
+            dma((groups,)),
+            dma((groups,)),
+            dma((2,)),
+        ],
+        compiler_params=pltpu.CompilerParams(collective_id=2, has_side_effects=True),
+    )(send_tiles, send_slots)
+
+
+def add_kernel(slots_ref, front_ref, got_ref, out_ref, sums):
+    groups, capacity, height, width = got_ref.shape
+    rows, cols = front_ref.shape
+    places = [
+        (slice(r * height, (r + 1) * height), slice(c * width, (c + 1) * width))
+        for r in range(rows // height)
+        for c in range(cols // width)
+    ]
+    for s, place in enumerate(places):
+        sums[s] = front_ref[place]
+
+    def add(g, carry):
+        for p in range(capacity):
+            s = slots_ref[g, 0, p]
+            sums[s] += got_ref[g, p].astype(jnp.float32)
+        return carry
+
+    lax.fori_loop(0, groups, add, 0, unroll=2)
+    for s, place in enumerate(places):
+        out_ref[place] = sums[s]
+
+
+def extend_add(front, got_tiles, got_slots):
+    smem = pl.BlockSpec(memory_space=pltpu.SMEM)
+    vmem = pl.BlockSpec(memory_space=pltpu.VMEM)
+    return pl.pallas_call(
+        add_kernel,
+        out_shape=jax.ShapeDtypeStruct(front.shape, front.dtype),
+        in_specs=[smem, vmem, vmem],
+        out_specs=vmem,
+        scratch_shapes=[pltpu.VMEM((EMPTY + 1,) + got_tiles.shape[2:], jnp.float32)],
+        compiler_params=pltpu.CompilerParams(vmem_limit_bytes=40 * 2**20),
+    )(got_slots, front, got_tiles)
+
+
 def local(front_matrix, child_tiles, dest_cube, dest_slot, diag_inverse):
-    cube_count = lax.axis_size("cube")
-    rows_local, cols_local = front_matrix.shape
     tile_count = child_tiles.shape[2]
-    tile_rows = child_tiles.shape[3]
-    tile_width = child_tiles.shape[4]
-    capacity = CAP
-    tile_cols = cols_local // tile_width
-    slots_local = rows_local // tile_rows * tile_cols
-    flat_tiles = child_tiles.reshape(tile_count, tile_rows * tile_width)
-    target = dest_cube.reshape(tile_count)
-    slot_ids = dest_slot.reshape(tile_count)
-    onehot = (target[:, None] == jnp.arange(cube_count, dtype=jnp.int32)[None, :]).astype(jnp.int32)
-    before = jnp.cumsum(onehot, axis=0) - onehot
-    position = jnp.sum(before * onehot, axis=1)
-    buffer_row = target * capacity + position
-    send_tiles = (
-        jnp.zeros((cube_count * capacity, tile_rows * tile_width), jnp.bfloat16)
-        .at[buffer_row]
-        .set(flat_tiles)
+    send_tiles, send_slots = pack(
+        dest_cube.reshape(tile_count),
+        dest_slot.reshape(tile_count),
+        child_tiles.reshape(child_tiles.shape[2:]),
+        lax.axis_size("cube"),
     )
-    send_slots = (
-        jnp.full((cube_count * capacity,), slots_local, jnp.int32).at[buffer_row].set(slot_ids)
-    )
-    got_tiles, got_slots = (
-        lax.all_to_all(
-            send_tiles.reshape(cube_count, capacity, tile_rows * tile_width),
-            "cube",
-            split_axis=0,
-            concat_axis=0,
-            tiled=True,
-        ),
-        lax.all_to_all(
-            send_slots.reshape(cube_count, capacity),
-            "cube",
-            split_axis=0,
-            concat_axis=0,
-            tiled=True,
-        ),
-    )
-    got_tiles = got_tiles.reshape(cube_count * capacity, tile_rows * tile_width)
-    got_slots = got_slots.reshape(cube_count * capacity)
-    select = (jnp.arange(slots_local, dtype=jnp.int32)[:, None] == got_slots[None, :]).astype(
-        jnp.bfloat16
-    )
-    extend_sum = jnp.dot(select, got_tiles, preferred_element_type=jnp.float32)
-    extend_sum = (
-        extend_sum.reshape(rows_local // tile_rows, tile_cols, tile_rows, tile_width)
-        .transpose(0, 2, 1, 3)
-        .reshape(rows_local, cols_local)
-    )
-    return spread(front_matrix + extend_sum, diag_inverse)
+    got_tiles, got_slots = exchange(send_tiles, send_slots)
+    return spread(extend_add(front_matrix, got_tiles, got_slots), diag_inverse)
 
 
 def solution(mesh):

time: 195 us -> 176 us (0.903)
  the two profiles are of different devices: /device:TPU:1 before, /device:TPU:17 now
where the time goes in v2:
time: 176 us
  Pallas kernels  168 us (95%)
  local copies, waits for them, and re-layouts  7.84 us (4%)
    pallas_call x1, Pallas kernels, exchange(): pl.pallas_call(exchange_kernel, out_shape=(jax.ShapeDtypeStruct(send_tile...  110 us
    pallas_call x1, Pallas kernels, spread(): pl.pallas_call(spread_kernel, out_shape=jax.ShapeDtypeStruct((rows, cols)...  54.1 us
    unnamed x19, local copies, waits for them, and re-layouts  7.84 us

profile of v2, /device:TPU:17, one launch (start us, length us, event | category | flops | bytes accessed | tf_op | source)
XLA Modules:
  0.0 175.7 jit_solution(12267520613180085530)
XLA Ops:
  0.0 0.0 copy-start.3
  0.0 1.2 copy-done.3
  1.2 0.0 copy-start.7
  1.2 0.7 copy-done.7
  1.9 0.0 copy-start.8
  1.9 0.7 copy-done.8
  2.5 1.4 shard_map.55
  3.9 0.0 copy-start
  4.0 1.3 copy-done
  5.3 0.0 copy-start.5
  5.3 0.6 copy-done.5
  5.9 0.0 copy-start.2
  5.9 109.6 %shard_map.56 = (bf16[64,4,32,128]{3,2,1,0:T(8,128)(2,1)}, s32[64,1,128]{2,1,0:T(1,128)}) custom-call(bf16[64,4,32,128]{3,2,1,0:T(8,128)(2,1)} %copy-done, s32[64,1,128]{2,1,0:T(1,128)} %copy-done.5), custom_call_target="tpu_custom_call" | custom-call | tf_op jit(solution)/shard_map/pallas_call | solution.py:343
  115.5 0.0 copy-done.2
  115.5 0.0 copy-start.1
  115.5 1.6 copy-done.1
  117.1 0.0 copy-start.6
  117.1 0.8 copy-done.6
  117.9 0.0 copy-start.4
  117.9 2.7 %shard_map.57.assembled_ref = f32[192,1536]{1,0:T(8,128)S(1)} custom-call(s32[64,1,128]{2,1,0:T(1,128)S(1)} %copy-done.6, f32[192,1536]{1,0:T(8,128)S(1)} %copy-done.2, bf16[64,4,32,128]{3,2,1,0:T(8,128)(2,1)S(1)} %copy-done.1), custom_call_target="tpu_custom_call" | custom-call | tf_op jit(solution)/shard_map/pallas_call | solution.py:387
  120.5 0.0 copy-done.4
  120.5 54.1 %shard_map.58 = f32[192,1536]{1,0:T(8,128)S(1)} custom-call(f32[192,1536]{1,0:T(8,128)S(1)} %shard_map.57.assembled_ref, bf16[512,512]{1,0:T(8,128)(2,1)S(1)} %copy-done.4), custom_call_target="tpu_custom_call" | custom-call | tf_op jit(solution)/shard_map/pallas_call | solution.py:216
  174.7 1.0 copy.7
Async XLA Ops:
  0.0 1.2 copy-start.3
  1.2 0.7 copy-start.7
  1.9 0.7 copy-start.8
  3.9 1.3 copy-start
  5.3 0.6 copy-start.5
  5.9 109.6 %copy-start.2 = (f32[192,1536]{1,0:T(8,128)S(1)}, f32[192,1536]{1,0:T(8,128)}, u32[]{:S(2)}) copy-start(f32[192,1536]{1,0:T(8,128)} %front_ref.1) | copy-start | bytes 3538948
  115.5 1.6 copy-start.1
  117.1 0.8 copy-start.6
  117.9 2.7 %copy-start.4 = (bf16[512,512]{1,0:T(8,128)(2,1)S(1)}, bf16[512,512]{1,0:T(8,128)(2,1)}, u32[]{:S(2)}) copy-start(bf16[512,512]{1,0:T(8,128)(2,1)} %diag_ref.1) | copy-start | bytes 1572868

commit v3 on v1

v3 whole, which is shorter than its diff:
```python
import functools

import jax
import jax.numpy as jnp
from jax import lax
from jax.experimental import pallas as pl
from jax.experimental.pallas import tpu as pltpu
from jax.sharding import PartitionSpec as P

CAP = 4
EMPTY = 72
HALF = 32
PARTS = 3
MESH = pl.DeviceIdType.MESH
QUARTERS = 4
MIDDLE = 4
BLOCKS = 8


def pack_kernel(cube_ref, slot_ref, tiles_ref, send_ref, slots_ref, counts):
    groups = send_ref.shape[0]
    place_from = (lax.axis_index("cube") % HALF) * CAP
    lane = lax.broadcasted_iota(jnp.int32, slots_ref.shape, 2)
    slots_ref[...] = jnp.where((lane >= place_from) & (lane < place_from + CAP), EMPTY, 0)
    lane = lax.broadcasted_iota(jnp.int32, (1, slots_ref.shape[2]), 1)

    def clear(g, carry):
        counts[g] = 0
        return carry

    lax.fori_loop(0, groups, clear, 0, unroll=8)

    def place(t, carry):
        g = cube_ref[t]
        p = counts[g]
        counts[g] = p + 1
        send_ref[g, p] = tiles_ref[t]
        slots_ref[g] = jnp.where(lane == place_from + p, slot_ref[t], slots_ref[g])
        return carry

    lax.fori_loop(0, tiles_ref.shape[0], place, 0, unroll=4)


def pack(target, slot_ids, tiles, groups):
    smem = pl.BlockSpec(memory_space=pltpu.SMEM)
    vmem = pl.BlockSpec(memory_space=pltpu.VMEM)
    return pl.pallas_call(
        pack_kernel,
        out_shape=(
            jax.ShapeDtypeStruct((groups, CAP) + tiles.shape[1:], tiles.dtype),
            jax.ShapeDtypeStruct((groups, 1, 128), jnp.int32),
        ),
        in_specs=[smem, smem, vmem],
        out_specs=(vmem, vmem),
        scratch_shapes=[pltpu.SMEM((groups,), jnp.int32)],
        compiler_params=pltpu.CompilerParams(vmem_limit_bytes=40 * 2**20),
    )(target, slot_ids, tiles)


def sort_table(row):
    count = row.shape[1]
    along = jnp.broadcast_to(row, (count, count))
    i = lax.broadcasted_iota(jnp.int32, (count, count), 0)
    j = lax.broadcasted_iota(jnp.int32, (count, count), 1)

    def total(mask, value, axis):
        return jnp.sum(jnp.where(mask, value, 0), axis=axis, keepdims=True)

    down = total(i == j, along, 1)
    earlier = (along == down) & (j < i)
    rank = total((along < down) | earlier, 1, 1)
    repeats = total(earlier, 1, 1)
    hit = rank == j
    return (
        total(hit, i, 0),
        total(hit & (repeats > 0), 1, 0),
        jnp.maximum(total(down <= j, 1, 0) - 1, 0),
        total(down == j, 1, 0),
    )


def front_kernel(
    send_ref,
    slots_ref,
    front_ref,
    diag_ref,
    out_ref,
    far_tiles,
    near_tiles,
    far_slots,
    near_slots,
    runs,
    table,
    order,
    dense,
    got_dense,
    own,
    across,
    table_sem,
    keep_sem,
    far_send,
    far_recv,
    far_slot_send,
    far_slot_recv,
    near_send,
    near_recv,
    near_slot_send,
    near_slot_recv,
    dense_send,
    dense_recv,
    own_recv,
    across_recv,
    down_send,
    cross_send,
    level_send,
    entry_send,
    chain_send,
    row_send,
    core_send,
):
    cube = lax.axis_index("cube")
    col = lax.axis_index("col")
    z = cube // 8
    x = (cube // 2) % 4
    core = cube % 2
    half = col // 4
    y = col % 4
    block = cube % 8
    near = cube % HALF
    base = cube - near
    mirror = cube ^ HALF
    rows, cols = front_ref.shape
    width = diag_ref.shape[0]
    depth = rows // QUARTERS
    tile_count, height, lanes = far_tiles.shape

    def at(z_to, x_to, core_to, half_to, y_to):
        return {"cube": z_to * 8 + x_to * 2 + core_to, "col": half_to * 4 + y_to}

    is_root = col == 0
    is_entry = (half == 0) & (y == z % 4)
    is_middle = z == MIDDLE
    has_above = z < 7
    has_below = z > 0
    level_peers = [at(z, x, core, half, (y + s) % 4) for s in (1, 2, 3)]
    half_peer = at(z, x, core, 1 - half, y)
    row_peers = [at(z, (x + s) % 4, core, half, y) for s in (1, 2, 3)]
    core_peer = at(z, x, 1 - core, half, y)
    above = at(z + 1, x, core, half, y)
    below = at(z - 1, x, core, half, y)
    entry_to = at(MIDDLE, x, core, z // 4, y)
    entry_from = at(half * 4 + y, x, core, 0, y)

    barrier = pltpu.get_barrier_semaphore()

    def greet(device):
        pl.semaphore_signal(barrier, inc=1, device_id=device, device_id_type=MESH)

    def near_peer(step):
        return base + (near ^ ((step % 4) * 8 + step // 4))

    def greet_near(step, carry):
        greet({"cube": near_peer(step)})
        return carry

    lax.fori_loop(1, HALF, greet_near, 0)
    for device in level_peers + [half_peer, {"cube": mirror}]:
        greet(device)
    for there, device in (
        (has_above, above),
        (has_below, below),
        (is_entry, entry_to),
        (is_middle, entry_from),
    ):
        pl.when(there)(functools.partial(greet, device))

    mine = pl.ds(near * CAP, CAP)
    kept = [
        pltpu.make_async_copy(send_ref.at[mirror], far_tiles.at[mine], keep_sem.at[0]),
        pltpu.make_async_copy(slots_ref.at[mirror], far_slots.at[near], keep_sem.at[1]),
        pltpu.make_async_copy(send_ref.at[cube], near_tiles.at[mine], keep_sem.at[2]),
        pltpu.make_async_copy(slots_ref.at[cube], near_slots.at[near], keep_sem.at[3]),
    ]
    for copy in kept:
        copy.start()

    pl.semaphore_wait(
        barrier,
        HALF
        + 4
        + has_above.astype(jnp.int32)
        + has_below.astype(jnp.int32)
        + is_entry.astype(jnp.int32)
        + is_middle.astype(jnp.int32),
    )

    def remote(source, target, send_sem, recv_sem, device):
        return pltpu.make_async_remote_copy(
            src_ref=source,
            dst_ref=target,
            send_sem=send_sem,
            recv_sem=recv_sem,
            device_id=device,
            device_id_type=MESH,
        )

    def far_copies(step):
        to = near_peer(step)
        device = {"cube": to}
        return (
            remote(
                slots_ref.at[to ^ HALF],
                far_slots.at[near],
                far_slot_send.at[step],
                far_slot_recv.at[step],
                device,
            ),
            remote(
                send_ref.at[to ^ HALF],
                far_tiles.at[mine],
                far_send.at[step],
                far_recv.at[step],
                device,
            ),
        )

    def near_copies(step):
        to = near_peer(step)
        device = {"cube": to}
        return (
            remote(
                slots_ref.at[to],
                near_slots.at[near],
                near_slot_send.at[step],
                near_slot_recv.at[step],
                device,
            ),
            remote(
                send_ref.at[to],
                near_tiles.at[mine],
                near_send.at[step],
                near_recv.at[step],
                device,
            ),
        )

    def each(copies, action):
        def body(step, carry):
            for copy in copies(step):
                getattr(copy, action)()
            return carry

        lax.fori_loop(1, HALF, body, 0)

    def sum_runs(slot_rows, tiles):
        for k, values in enumerate(sort_table(jnp.sum(slot_rows[...], axis=0))):
            table[k : k + 1] = values
        copy = pltpu.make_async_copy(table, order, table_sem.at[0])
        copy.start()
        copy.wait()

        def add(rank, run):
            tile = tiles[order[0, rank]].astype(jnp.float32)
            run = tile + jnp.where(order[1, rank] > 0, run, 0.0)
            runs[rank] = run
            return run

        lax.fori_loop(
            0, tile_count, add, jnp.zeros((height, lanes), jnp.float32), unroll=8
        )

    def block_sum(s):
        return jnp.where(order[3, s] > 0, runs[order[2, s]], 0.0)

    each(far_copies, "start")
    each(far_copies, "wait_recv")
    kept[0].wait()
    kept[1].wait()
    each(near_copies, "start")

    sum_runs(far_slots, far_tiles)
    per_row = cols // lanes
    group = width // lanes
    tile_rows = rows // height
    dense_copies = []
    for part in range(PARTS):

        def fill(r, carry):
            for c in range(group):
                dense[part, r * group + c] = block_sum(r * per_row + part * group + c).astype(
                    jnp.bfloat16
                )
            return carry

        lax.fori_loop(0, tile_rows, fill, 0, unroll=2)
        copy = remote(
            dense.at[part],
            got_dense.at[part],
            dense_send.at[part],
            dense_recv.at[part],
            {"cube": mirror},
        )
        copy.start()
        dense_copies.append(copy)

    each(near_copies, "wait_recv")
    kept[2].wait()
    kept[3].wait()
    sum_runs(near_slots, near_tiles)

    def assemble(part):
        dense_copies[part].wait_recv()

        def fill(r, carry):
            for c in range(group):
                here = (
                    pl.ds(pl.multiple_of(r * height, height), height),
                    pl.ds((part * group + c) * lanes, lanes),
                )
                out_ref[here] = (
                    front_ref[here]
                    + block_sum(r * per_row + part * group + c)
                    + got_dense[part, r * group + c].astype(jnp.float32)
                )
            return carry

        lax.fori_loop(0, tile_rows, fill, 0, unroll=2)

    assemble(0)

    @pl.when(is_root)
    def _():
        panel = jnp.dot(
            out_ref[:, :width].astype(jnp.bfloat16),
            diag_ref[...],
            preferred_element_type=jnp.float32,
        ).astype(jnp.bfloat16)
        for q in range(QUARTERS):
            own[q] = panel[q * depth : (q + 1) * depth]

    started = []

    def send(there, source, target, send_sem, recv_sem, device):
        copy = remote(source, target, send_sem, recv_sem, device)
        if there is None:
            copy.start()
        else:
            pl.when(there)(copy.start)
        started.append((there, copy))

    def arrived(target, recv_sem):
        remote(target, target, recv_sem, recv_sem, core_peer).wait_recv()

    first = jnp.maximum(z % 4 - 1, 0)
    for s in range(3):
        y_to = 1 + (first + s) % 3
        for q in range(QUARTERS):
            send(
                is_root,
                own.at[q],
                own.at[q],
                down_send.at[s * QUARTERS + q],
                own_recv.at[q],
                at(z, x, core, 0, y_to),
            )

    for q in range(QUARTERS):
        pl.when((half == 0) & (y != 0))(functools.partial(arrived, own.at[q], own_recv.at[q]))
        send(
            is_entry,
            own.at[q],
            across.at[block, q],
            entry_send.at[q],
            across_recv.at[block, q],
            entry_to,
        )
    send(half == 0, own.at[y], own.at[y], cross_send.at[0], own_recv.at[y], half_peer)

    for q in range(QUARTERS + 1):
        if q < QUARTERS:
            arrived(across.at[block, q], across_recv.at[block, q])
            held = (across.at[block, q], across.at[block, q])
            ready = across_recv.at[block, q]
            send(has_above & (z >= MIDDLE), *held, chain_send.at[q, 0], ready, above)
            send(has_below & (z <= MIDDLE), *held, chain_send.at[q, 1], ready, below)
            for s in range(3):
                send(None, *held, row_send.at[q, s], ready, row_peers[s])
            send(None, *held, core_send.at[q, 0], ready, core_peer)
        if q == 2:
            pl.when(half == 1)(functools.partial(arrived, own.at[y], own_recv.at[y]))
            for s in range(3):
                send(
                    half == 1,
                    own.at[y],
                    own.at[y],
                    level_send.at[s],
                    own_recv.at[y],
                    level_peers[s],
                )
        if q > 0:
            for s in range(3):
                theirs = ((x + s + 1) % 4) * 2 + core
                arrived(across.at[theirs, q - 1], across_recv.at[theirs, q - 1])
                send(
                    None,
                    across.at[theirs, q - 1],
                    across.at[theirs, q - 1],
                    core_send.at[q - 1, s + 1],
                    across_recv.at[theirs, q - 1],
                    core_peer,
                )

    for part in range(1, PARTS):
        assemble(part)
    for s in range(1, QUARTERS):
        q = (y + s) % 4
        pl.when(half == 1)(functools.partial(arrived, own.at[q], own_recv.at[q]))
    for q in range(QUARTERS):
        for s in range(4):
            theirs = s * 2 + 1 - core
            arrived(across.at[theirs, q], across_recv.at[theirs, q])

    panel = own[...].reshape(rows, width)
    span = cols // 4
    for s in range(4):
        part = across[2 * s : 2 * s + 2].reshape(span, width)
        update = lax.dot_general(
            panel, part, (((1,), (1,)), ((), ())), preferred_element_type=jnp.float32
        )
        here = slice(s * span, (s + 1) * span)
        out_ref[:, here] = out_ref[:, here] - update

    @pl.when(is_root)
    def _():
        out_ref[:, :width] = panel.astype(jnp.float32)

    each(far_copies, "wait_send")
    each(near_copies, "wait_send")
    for copy in dense_copies:
        copy.wait_send()
    for there, copy in started:
        if there is None:
            copy.wait_send()
        else:
            pl.when(there)(copy.wait_send)


def factor(send_tiles, send_slots, front, diag_inverse):
    rows, cols = front.shape
    width = diag_inverse.shape[0]
    depth = rows // QUARTERS
    tile = send_tiles.shape[2:]
    vmem = pl.BlockSpec(memory_space=pltpu.VMEM)
    dma = pltpu.SemaphoreType.DMA
    return pl.pallas_call(
        front_kernel,
        out_shape=jax.ShapeDtypeStruct((rows, cols), jnp.float32),
        in_specs=[vmem, vmem, vmem, vmem],
        out_specs=vmem,
        scratch_shapes=[
            pltpu.VMEM((HALF * CAP,) + tile, jnp.bfloat16),
            pltpu.VMEM((HALF * CAP,) + tile, jnp.bfloat16),
            pltpu.VMEM((HALF, 1, 128), jnp.int32),
            pltpu.VMEM((HALF, 1, 128), jnp.int32),
            pltpu.VMEM((HALF * CAP,) + tile, jnp.float32),
            pltpu.VMEM((8, 128), jnp.int32),
            pltpu.SMEM((8, 128), jnp.int32),
            pltpu.VMEM((PARTS, EMPTY // PARTS) + tile, jnp.bfloat16),
            pltpu.VMEM((PARTS, EMPTY // PARTS) + tile, jnp.bfloat16),
            pltpu.VMEM((QUARTERS, depth, width), jnp.bfloat16),
            pltpu.VMEM((BLOCKS, QUARTERS, depth, width), jnp.bfloat16),
            dma((1,)),
            dma((4,)),
            dma((HALF,)),
            dma((HALF,)),
            dma((HALF,)),
            dma((HALF,)),
            dma((HALF,)),
            dma((HALF,)),
            dma((HALF,)),
            dma((HALF,)),
            dma((PARTS,)),
            dma((PARTS,)),
            dma((QUARTERS,)),
            dma((BLOCKS, QUARTERS)),
            dma((3 * QUARTERS,)),
            dma((1,)),
            dma((3,)),
            dma((QUARTERS,)),
            dma((QUARTERS, 2)),
            dma((QUARTERS, 3)),
            dma((QUARTERS, 4)),
        ],
        compiler_params=pltpu.CompilerParams(
            collective_id=1, has_side_effects=True, vmem_limit_bytes=48 * 2**20
        ),
    )(send_tiles, send_slots, front, diag_inverse)


def local(front_matrix, child_tiles, dest_cube, dest_slot, diag_inverse):
    tile_count = child_tiles.shape[2]
    send_tiles, send_slots = pack(
        dest_cube.reshape(tile_count),
        dest_slot.reshape(tile_count),
        child_tiles.reshape(child_tiles.shape[2:]),
        lax.axis_size("cube"),
    )
    return factor(send_tiles, send_slots, front_matrix, diag_inverse)


def solution(mesh):
    in_specs = (
        P("cube", "col"),
        P("cube", "col", None, None, None),
        P("cube", "col", None, None),
        P("cube", "col", None),
        P(),
    )
    out_specs = P("cube", "col")
    return jax.shard_map(local, mesh=mesh, in_specs=in_specs, out_specs=out_specs, check_vma=False)
```

time: 195 us -> 140 us (0.72)
  the two profiles are of different devices: /device:TPU:1 before, /device:TPU:25 now
where the time goes in v3:
time: 140 us
  Pallas kernels  135 us (96%)
  local copies, waits for them, and re-layouts  4.82 us (3%)
    pallas_call x1, Pallas kernels, factor(): pl.pallas_call(front_kernel, out_shape=jax.ShapeDtypeStruct((rows, cols),...  133 us
    unnamed x11, local copies, waits for them, and re-layouts  4.82 us

profile of v3, /device:TPU:25, one launch (start us, length us, event | category | flops | bytes accessed | tf_op | source)
XLA Modules:
  0.0 139.6 jit_solution(18352641029895293898)
XLA Ops:
  0.0 0.0 copy-start.1
  0.0 1.2 copy-done.1
  1.2 0.0 copy-start.3
  1.2 0.7 copy-done.3
  1.9 0.0 copy-start.4
  1.9 0.7 copy-done.4
  2.5 0.0 copy-start.2
  2.5 1.5 %shard_map.55 = (bf16[64,4,32,128]{3,2,1,0:T(8,128)(2,1)S(1)}, s32[64,1,128]{2,1,0:T(1,128)S(1)}) custom-call(s32[128]{0:T(128)S(1)} %bitcast.4, s32[128]{0:T(128)S(1)} %bitcast.5, bf16[128,32,128]{2,1,0:T(8,128)(2,1)S(1)} %bitcast.3), custom_call_target="tpu_custom_call" | custom-call | tf_op jit(solution)/shard_map/pallas_call | solution.py:47
  4.0 0.0 copy-done.2
  4.0 0.0 copy-start
  4.0 1.3 copy-done
  5.3 133.3 %shard_map.56 = f32[192,1536]{1,0:T(8,128)S(1)} custom-call(bf16[64,4,32,128]{3,2,1,0:T(8,128)(2,1)S(1)} %get-tuple-element.7.send_ref, s32[64,1,128]{2,1,0:T(1,128)S(1)} %get-tuple-element.8.slots_ref, f32[192,1536]{1,0:T(8,128)S(1)} %copy-done, bf16[512,512]{1,0:T(8,128)(2,1)S(1)} %copy-done.2), custom_call_target="tpu_custom_call" | custom-call | tf_op jit(solution)/shard_map/pallas_call | solution.py:455
  138.6 1.0 copy.7
Async XLA Ops:
  0.0 1.2 copy-start.1
  1.2 0.7 copy-start.3
  1.9 0.7 copy-start.4
  2.5 1.5 %copy-start.2 = (bf16[512,512]{1,0:T(8,128)(2,1)S(1)}, bf16[512,512]{1,0:T(8,128)(2,1)}, u32[]{:S(2)}) copy-start(bf16[512,512]{1,0:T(8,128)(2,1)} %diag_ref.1) | copy-start | bytes 1572868
  4.0 1.3 copy-start

commit v4 on v3

--- a/solution.py
+++ b/solution.py
@@ -12,8 +12,10 @@
 HALF = 32
 PARTS = 3
 MESH = pl.DeviceIdType.MESH
-QUARTERS = 4
-MIDDLE = 4
+PIECES = 4
+BURST = 4
+EARLY = 2
+LATE = 2
 BLOCKS = 8
 
 
@@ -114,7 +116,7 @@
     cross_send,
     level_send,
     entry_send,
-    chain_send,
+    line_send,
     row_send,
     core_send,
 ):
@@ -131,7 +133,7 @@
     mirror = cube ^ HALF
     rows, cols = front_ref.shape
     width = diag_ref.shape[0]
-    depth = rows // QUARTERS
+    depth = rows // PIECES
     tile_count, height, lanes = far_tiles.shape
 
     def at(z_to, x_to, core_to, half_to, y_to):
@@ -139,16 +141,16 @@
 
     is_root = col == 0
     is_entry = (half == 0) & (y == z % 4)
-    is_middle = z == MIDDLE
-    has_above = z < 7
-    has_below = z > 0
+    line = z - z % 4
+    is_hub = z == jnp.where(z < 4, 2 - (col == 2).astype(jnp.int32), 5)
     level_peers = [at(z, x, core, half, (y + s) % 4) for s in (1, 2, 3)]
     half_peer = at(z, x, core, 1 - half, y)
     row_peers = [at(z, (x + s) % 4, core, half, y) for s in (1, 2, 3)]
     core_peer = at(z, x, 1 - core, half, y)
-    above = at(z + 1, x, core, half, y)
-    below = at(z - 1, x, core, half, y)
-    entry_to = at(MIDDLE, x, core, z // 4, y)
+    line_peers = [at(line + (z + s) % 4, x, core, half, y) for s in (1, 2, 3)]
+    entry_to = [
+        at(hub, x, core, z // 4, y) for hub in (2 - (z == 2).astype(jnp.int32), 5)
+    ]
     entry_from = at(half * 4 + y, x, core, 0, y)
 
     barrier = pltpu.get_barrier_semaphore()
@@ -167,10 +169,9 @@
     for device in level_peers + [half_peer, {"cube": mirror}]:
         greet(device)
     for there, device in (
-        (has_above, above),
-        (has_below, below),
-        (is_entry, entry_to),
-        (is_middle, entry_from),
+        (is_entry, entry_to[0]),
+        (is_entry, entry_to[1]),
+        (is_hub, entry_from),
     ):
         pl.when(there)(functools.partial(greet, device))
 
@@ -180,6 +181,7 @@
         pltpu.make_async_copy(slots_ref.at[mirror], far_slots.at[near], keep_sem.at[1]),
         pltpu.make_async_copy(send_ref.at[cube], near_tiles.at[mine], keep_sem.at[2]),
         pltpu.make_async_copy(slots_ref.at[cube], near_slots.at[near], keep_sem.at[3]),
+        pltpu.make_async_copy(front_ref, out_ref, keep_sem.at[4]),
     ]
     for copy in kept:
         copy.start()
@@ -188,10 +190,8 @@
         barrier,
         HALF
         + 4
-        + has_above.astype(jnp.int32)
-        + has_below.astype(jnp.int32)
-        + is_entry.astype(jnp.int32)
-        + is_middle.astype(jnp.int32),
+        + 2 * is_entry.astype(jnp.int32)
+        + is_hub.astype(jnp.int32),
     )
 
     def remote(source, target, send_sem, recv_sem, device):
@@ -282,6 +282,7 @@
     per_row = cols // lanes
     group = width // lanes
     tile_rows = rows // height
+    bursts = dense.shape[1] // BURST
     dense_copies = []
     for part in range(PARTS):
 
@@ -293,23 +294,29 @@
             return carry
 
         lax.fori_loop(0, tile_rows, fill, 0, unroll=2)
-        copy = remote(
-            dense.at[part],
-            got_dense.at[part],
-            dense_send.at[part],
-            dense_recv.at[part],
-            {"cube": mirror},
-        )
-        copy.start()
-        dense_copies.append(copy)
+        for k in range(bursts):
+            here = pl.ds(k * BURST, BURST)
+            dense_copies.append(
+                remote(
+                    dense.at[part, here],
+                    got_dense.at[part, here],
+                    dense_send.at[part, k],
+                    dense_recv.at[part, k],
+                    {"cube": mirror},
+                )
+            )
+            if part < EARLY:
+                dense_copies[-1].start()
 
     each(near_copies, "wait_recv")
     kept[2].wait()
     kept[3].wait()
+    kept[4].wait()
     sum_runs(near_slots, near_tiles)
 
     def assemble(part):
-        dense_copies[part].wait_recv()
+        for copy in dense_copies[part * bursts : (part + 1) * bursts]:
+            copy.wait_recv()
 
         def fill(r, carry):
             for c in range(group):
@@ -318,7 +325,7 @@
                     pl.ds((part * group + c) * lanes, lanes),
                 )
                 out_ref[here] = (
-                    front_ref[here]
+                    out_ref[here]
                     + block_sum(r * per_row + part * group + c)
                     + got_dense[part, r * group + c].astype(jnp.float32)
                 )
@@ -335,7 +342,7 @@
             diag_ref[...],
             preferred_element_type=jnp.float32,
         ).astype(jnp.bfloat16)
-        for q in range(QUARTERS):
+        for q in range(PIECES):
             own[q] = panel[q * depth : (q + 1) * depth]
 
     started = []
@@ -354,68 +361,84 @@
     first = jnp.maximum(z % 4 - 1, 0)
     for s in range(3):
         y_to = 1 + (first + s) % 3
-        for q in range(QUARTERS):
+        for q in range(PIECES):
             send(
                 is_root,
                 own.at[q],
                 own.at[q],
-                down_send.at[s * QUARTERS + q],
+                down_send.at[s, q],
                 own_recv.at[q],
                 at(z, x, core, 0, y_to),
             )
 
-    for q in range(QUARTERS):
-        pl.when((half == 0) & (y != 0))(functools.partial(arrived, own.at[q], own_recv.at[q]))
-        send(
-            is_entry,
-            own.at[q],
-            across.at[block, q],
-            entry_send.at[q],
-            across_recv.at[block, q],
-            entry_to,
-        )
-    send(half == 0, own.at[y], own.at[y], cross_send.at[0], own_recv.at[y], half_peer)
-
-    for q in range(QUARTERS + 1):
-        if q < QUARTERS:
-            arrived(across.at[block, q], across_recv.at[block, q])
+    for q in range(PIECES):
+        pl.when(is_entry & (y != 0))(functools.partial(arrived, own.at[q], own_recv.at[q]))
+        for k in range(2):
+            send(
+                is_entry,
+                own.at[q],
+                across.at[block, q],
+                entry_send.at[q, k],
+                across_recv.at[block, q],
+                entry_to[k],
+            )
+
+    for step in range(PIECES + 1):
+        q = step
+        if q < PIECES:
+            ready = across_recv.at[block, q]
+            arrived(across.at[block, q], ready)
             held = (across.at[block, q], across.at[block, q])
-            ready = across_recv.at[block, q]
-            send(has_above & (z >= MIDDLE), *held, chain_send.at[q, 0], ready, above)
-            send(has_below & (z <= MIDDLE), *held, chain_send.at[q, 1], ready, below)
+            for s in range(3):
+                send(is_hub, *held, line_send.at[q, s], ready, line_peers[s])
             for s in range(3):
                 send(None, *held, row_send.at[q, s], ready, row_peers[s])
             send(None, *held, core_send.at[q, 0], ready, core_peer)
-        if q == 2:
-            pl.when(half == 1)(functools.partial(arrived, own.at[y], own_recv.at[y]))
-            for s in range(3):
-                send(
-                    half == 1,
-                    own.at[y],
-                    own.at[y],
-                    level_send.at[s],
-                    own_recv.at[y],
-                    level_peers[s],
-                )
-        if q > 0:
+        q = step - 1
+        if q >= 0:
             for s in range(3):
                 theirs = ((x + s + 1) % 4) * 2 + core
-                arrived(across.at[theirs, q - 1], across_recv.at[theirs, q - 1])
+                ready = across_recv.at[theirs, q]
+                arrived(across.at[theirs, q], ready)
+                held = (across.at[theirs, q], across.at[theirs, q])
+                send(None, *held, core_send.at[q, s + 1], ready, core_peer)
+        for copy in dense_copies[EARLY * bursts + step * LATE : EARLY * bursts + (step + 1) * LATE]:
+            copy.start()
+        if step == 2:
+            for q in range(PIECES):
+                pl.when((half == 0) & (y != 0) & jnp.logical_not(is_entry))(
+                    functools.partial(arrived, own.at[q], own_recv.at[q])
+                )
+            for q in range(PIECES):
                 send(
-                    None,
-                    across.at[theirs, q - 1],
-                    across.at[theirs, q - 1],
-                    core_send.at[q - 1, s + 1],
-                    across_recv.at[theirs, q - 1],
-                    core_peer,
+                    (half == 0) & (y == q % 4),
+                    own.at[q],
+                    own.at[q],
+                    cross_send.at[q],
+                    own_recv.at[q],
+                    half_peer,
                 )
+        if step == PIECES:
+            for q in range(PIECES):
+                holds = (half == 1) & (y == q % 4)
+                pl.when(holds)(functools.partial(arrived, own.at[q], own_recv.at[q]))
+                for s in range(3):
+                    send(
+                        holds,
+                        own.at[q],
+                        own.at[q],
+                        level_send.at[q, s],
+                        own_recv.at[q],
+                        level_peers[s],
+                    )
 
     for part in range(1, PARTS):
         assemble(part)
-    for s in range(1, QUARTERS):
-        q = (y + s) % 4
-        pl.when(half == 1)(functools.partial(arrived, own.at[q], own_recv.at[q]))
-    for q in range(QUARTERS):
+    for q in range(PIECES):
+        pl.when((half == 1) & (y != q % 4))(
+            functools.partial(arrived, own.at[q], own_recv.at[q])
+        )
+    for q in range(PIECES):
         for s in range(4):
             theirs = s * 2 + 1 - core
             arrived(across.at[theirs, q], across_recv.at[theirs, q])
@@ -448,14 +471,14 @@
 def factor(send_tiles, send_slots, front, diag_inverse):
     rows, cols = front.shape
     width = diag_inverse.shape[0]
-    depth = rows // QUARTERS
+    depth = rows // PIECES
     tile = send_tiles.shape[2:]
     vmem = pl.BlockSpec(memory_space=pltpu.VMEM)
     dma = pltpu.SemaphoreType.DMA
     return pl.pallas_call(
         front_kernel,
         out_shape=jax.ShapeDtypeStruct((rows, cols), jnp.float32),
-        in_specs=[vmem, vmem, vmem, vmem],
+        in_specs=[vmem, vmem, pl.BlockSpec(memory_space=pl.ANY), vmem],
         out_specs=vmem,
         scratch_shapes=[
             pltpu.VMEM((HALF * CAP,) + tile, jnp.bfloat16),
@@ -467,29 +490,29 @@
             pltpu.SMEM((8, 128), jnp.int32),
             pltpu.VMEM((PARTS, EMPTY // PARTS) + tile, jnp.bfloat16),
             pltpu.VMEM((PARTS, EMPTY // PARTS) + tile, jnp.bfloat16),
-            pltpu.VMEM((QUARTERS, depth, width), jnp.bfloat16),
-            pltpu.VMEM((BLOCKS, QUARTERS, depth, width), jnp.bfloat16),
+            pltpu.VMEM((PIECES, depth, width), jnp.bfloat16),
+            pltpu.VMEM((BLOCKS, PIECES, depth, width), jnp.bfloat16),
             dma((1,)),
-            dma((4,)),
-            dma((HALF,)),
-            dma((HALF,)),
-            dma((HALF,)),
-            dma((HALF,)),
-            dma((HALF,)),
-            dma((HALF,)),
-            dma((HALF,)),
-            dma((HALF,)),
-            dma((PARTS,)),
-            dma((PARTS,)),
-            dma((QUARTERS,)),
-            dma((BLOCKS, QUARTERS)),
-            dma((3 * QUARTERS,)),
-            dma((1,)),
-            dma((3,)),
-            dma((QUARTERS,)),
-            dma((QUARTERS, 2)),
-            dma((QUARTERS, 3)),
-            dma((QUARTERS, 4)),
+            dma((5,)),
+            dma((HALF,)),
+            dma((HALF,)),
+            dma((HALF,)),
+            dma((HALF,)),
+            dma((HALF,)),
+            dma((HALF,)),
+            dma((HALF,)),
+            dma((HALF,)),
+            dma((PARTS, EMPTY // PARTS // BURST)),
+            dma((PARTS, EMPTY // PARTS // BURST)),
+            dma((PIECES,)),
+            dma((BLOCKS, PIECES)),
+            dma((3, PIECES)),
+            dma((PIECES,)),
+            dma((PIECES, 3)),
+            dma((PIECES, 2)),
+            dma((PIECES, 3)),
+            dma((PIECES, 3)),
+            dma((PIECES, 4)),
         ],
         compiler_params=pltpu.CompilerParams(
             collective_id=1, has_side_effects=True, vmem_limit_bytes=48 * 2**20

time: 140 us -> 128 us (0.914)
  the two profiles are of different devices: /device:TPU:25 before, /device:TPU:384 now
where the time goes in v4:
time: 128 us
  Pallas kernels  123 us (96%)
  local copies, waits for them, and re-layouts  4.82 us (4%)
    pallas_call x1, Pallas kernels, factor(): pl.pallas_call(front_kernel, out_shape=jax.ShapeDtypeStruct((rows, cols),...  121 us
    unnamed x11, local copies, waits for them, and re-layouts  4.82 us

profile of v4, /device:TPU:384, one launch (start us, length us, event | category | flops | bytes accessed | tf_op | source)
XLA Modules:
  0.0 127.6 jit_solution(12271011006974977477)
XLA Ops:
  0.0 0.0 copy-start.1
  0.0 1.2 copy-done.1
  1.2 0.0 copy-start.3
  1.2 0.7 copy-done.3
  1.9 0.0 copy-start.4
  1.9 0.7 copy-done.4
  2.5 0.0 copy-start.2
  2.5 1.5 %shard_map.55 = (bf16[64,4,32,128]{3,2,1,0:T(8,128)(2,1)S(1)}, s32[64,1,128]{2,1,0:T(1,128)S(1)}) custom-call(s32[128]{0:T(128)S(1)} %bitcast.4, s32[128]{0:T(128)S(1)} %bitcast.5, bf16[128,32,128]{2,1,0:T(8,128)(2,1)S(1)} %bitcast.3), custom_call_target="tpu_custom_call" | custom-call | tf_op jit(solution)/shard_map/pallas_call | solution.py:49
  4.0 0.0 copy-done.2
  4.0 0.0 copy-start
  4.0 1.3 copy-done
  5.3 121.3 %shard_map.56 = f32[192,1536]{1,0:T(8,128)S(1)} custom-call(bf16[64,4,32,128]{3,2,1,0:T(8,128)(2,1)S(1)} %get-tuple-element.7.send_ref, s32[64,1,128]{2,1,0:T(1,128)S(1)} %get-tuple-element.8.slots_ref, f32[192,1536]{1,0:T(8,128)S(1)} %copy-done, bf16[512,512]{1,0:T(8,128)(2,1)S(1)} %copy-done.2), custom_call_target="tpu_custom_call" | custom-call | tf_op jit(solution)/shard_map/pallas_call | solution.py:478
  126.6 1.0 copy.7
Async XLA Ops:
  0.0 1.2 copy-start.1
  1.2 0.7 copy-start.3
  1.9 0.7 copy-start.4
  2.5 1.5 %copy-start.2 = (bf16[512,512]{1,0:T(8,128)(2,1)S(1)}, bf16[512,512]{1,0:T(8,128)(2,1)}, u32[]{:S(2)}) copy-start(bf16[512,512]{1,0:T(8,128)(2,1)} %diag_ref.1) | copy-start | bytes 1572868
  4.0 1.3 copy-start

commit v5 on v4

--- a/solution.py
+++ b/solution.py
@@ -12,10 +12,15 @@
 HALF = 32
 PARTS = 3
 MESH = pl.DeviceIdType.MESH
-PIECES = 4
+PIECES = 6
 BURST = 4
-EARLY = 2
+EARLY = 12
 LATE = 2
+LATE_STEP = 0
+ORDER = 1
+CROSS_STEP = 2
+LEVEL_STEP = 6
+WAVES = 1
 BLOCKS = 8
 
 
@@ -158,8 +163,14 @@
     def greet(device):
         pl.semaphore_signal(barrier, inc=1, device_id=device, device_id_type=MESH)
 
-    def near_peer(step):
-        return base + (near ^ ((step % 4) * 8 + step // 4))
+    def near_peer(apart):
+        return base + (near ^ apart)
+
+    def apart_at(place):
+        if not WAVES:
+            return ((place + 1) % 4) * 8 + (place + 1) // 4
+        place = place + jnp.where(core == 0, 1, place // 16)
+        return (place % 4) * 8 + (place // 4 % 4) * 2 + (core ^ (place // 16))
 
     def greet_near(step, carry):
         greet({"cube": near_peer(step)})
@@ -245,12 +256,12 @@
         )
 
     def each(copies, action):
-        def body(step, carry):
-            for copy in copies(step):
+        def body(place, carry):
+            for copy in copies(apart_at(place)):
                 getattr(copy, action)()
             return carry
 
-        lax.fori_loop(1, HALF, body, 0)
+        lax.fori_loop(0, HALF - 1, body, 0)
 
     def sum_runs(slot_rows, tiles):
         for k, values in enumerate(sort_table(jnp.sum(slot_rows[...], axis=0))):
@@ -276,7 +287,8 @@
     each(far_copies, "wait_recv")
     kept[0].wait()
     kept[1].wait()
-    each(near_copies, "start")
+    if ORDER == 0:
+        each(near_copies, "start")
 
     sum_runs(far_slots, far_tiles)
     per_row = cols // lanes
@@ -305,8 +317,10 @@
                     {"cube": mirror},
                 )
             )
-            if part < EARLY:
+            if part * bursts + k < EARLY:
                 dense_copies[-1].start()
+        if part + 1 == ORDER:
+            each(near_copies, "start")
 
     each(near_copies, "wait_recv")
     kept[2].wait()
@@ -402,9 +416,11 @@
                 arrived(across.at[theirs, q], ready)
                 held = (across.at[theirs, q], across.at[theirs, q])
                 send(None, *held, core_send.at[q, s + 1], ready, core_peer)
-        for copy in dense_copies[EARLY * bursts + step * LATE : EARLY * bursts + (step + 1) * LATE]:
-            copy.start()
-        if step == 2:
+        if step >= LATE_STEP:
+            late = EARLY + (step - LATE_STEP) * LATE
+            for copy in dense_copies[late : late + LATE]:
+                copy.start()
+        if step == CROSS_STEP:
             for q in range(PIECES):
                 pl.when((half == 0) & (y != 0) & jnp.logical_not(is_entry))(
                     functools.partial(arrived, own.at[q], own_recv.at[q])
@@ -418,7 +434,7 @@
                     own_recv.at[q],
                     half_peer,
                 )
-        if step == PIECES:
+        if step == LEVEL_STEP:
             for q in range(PIECES):
                 holds = (half == 1) & (y == q % 4)
                 pl.when(holds)(functools.partial(arrived, own.at[q], own_recv.at[q]))

time: 128 us -> 128 us (level)
  the two profiles are of different devices: /device:TPU:384 before, /device:TPU:1 now
where the time goes in v5:
time: 128 us; the launch traced here: 127 us
  Pallas kernels  123 us (96%)
  local copies, waits for them, and re-layouts  4.82 us (4%)
    pallas_call x1, Pallas kernels, factor(): pl.pallas_call(front_kernel, out_shape=jax.ShapeDtypeStruct((rows, cols),...  121 us
    unnamed x11, local copies, waits for them, and re-layouts  4.82 us

profile of v5, /device:TPU:1, one launch (start us, length us, event | category | flops | bytes accessed | tf_op | source)
XLA Modules:
  0.0 127.4 jit_solution(15305548291837910882)
XLA Ops:
  0.0 0.0 copy-start.1
  0.0 1.2 copy-done.1
  1.2 0.0 copy-start.3
  1.2 0.7 copy-done.3
  1.9 0.0 copy-start.4
  1.9 0.7 copy-done.4
  2.5 0.0 copy-start.2
  2.5 1.5 %shard_map.55 = (bf16[64,4,32,128]{3,2,1,0:T(8,128)(2,1)S(1)}, s32[64,1,128]{2,1,0:T(1,128)S(1)}) custom-call(s32[128]{0:T(128)S(1)} %bitcast.4, s32[128]{0:T(128)S(1)} %bitcast.5, bf16[128,32,128]{2,1,0:T(8,128)(2,1)S(1)} %bitcast.3), custom_call_target="tpu_custom_call" | custom-call | tf_op jit(solution)/shard_map/pallas_call | solution.py:54
  4.0 0.0 copy-done.2
  4.0 0.0 copy-start
  4.0 1.3 copy-done
  5.3 121.1 %shard_map.56 = f32[192,1536]{1,0:T(8,128)S(1)} custom-call(bf16[64,4,32,128]{3,2,1,0:T(8,128)(2,1)S(1)} %get-tuple-element.7.send_ref, s32[64,1,128]{2,1,0:T(1,128)S(1)} %get-tuple-element.8.slots_ref, f32[192,1536]{1,0:T(8,128)S(1)} %copy-done, bf16[512,512]{1,0:T(8,128)(2,1)S(1)} %copy-done.2), custom_call_target="tpu_custom_call" | custom-call | tf_op jit(solution)/shard_map/pallas_call | solution.py:494
  126.4 1.0 copy.7
Async XLA Ops:
  0.0 1.2 copy-start.1
  1.2 0.7 copy-start.3
  1.9 0.7 copy-start.4
  2.5 1.5 %copy-start.2 = (bf16[512,512]{1,0:T(8,128)(2,1)S(1)}, bf16[512,512]{1,0:T(8,128)(2,1)}, u32[]{:S(2)}) copy-start(bf16[512,512]{1,0:T(8,128)(2,1)} %diag_ref.1) | copy-start | bytes 1572868
  4.0 1.3 copy-start

commit v6 on v5

--- a/solution.py
+++ b/solution.py
@@ -397,6 +397,7 @@
                 entry_to[k],
             )
 
+    assemble(1)
     for step in range(PIECES + 1):
         q = step
         if q < PIECES:
@@ -448,7 +449,7 @@
                         level_peers[s],
                     )
 
-    for part in range(1, PARTS):
+    for part in range(2, PARTS):
         assemble(part)
     for q in range(PIECES):
         pl.when((half == 1) & (y != q % 4))(

time: 128 us -> 130 us (1.016)
  no operation moved by 1% of the time
where the time goes in v6:
time: 130 us; the launch traced here: 129 us
  Pallas kernels  124 us (95%)
  local copies, waits for them, and re-layouts  4.82 us (4%)
    pallas_call x1, Pallas kernels, factor(): pl.pallas_call(front_kernel, out_shape=jax.ShapeDtypeStruct((rows, cols),...  122 us
    unnamed x11, local copies, waits for them, and re-layouts  4.82 us

profile of v6, /device:TPU:1, one launch (start us, length us, event | category | flops | bytes accessed | tf_op | source)
XLA Modules:
  0.0 128.7 jit_solution(15521539759451956408)
XLA Ops:
  0.0 0.0 copy-start.1
  0.0 1.2 copy-done.1
  1.2 0.0 copy-start.3
  1.2 0.7 copy-done.3
  1.9 0.0 copy-start.4
  1.9 0.7 copy-done.4
  2.5 0.0 copy-start.2
  2.5 1.5 %shard_map.55 = (bf16[64,4,32,128]{3,2,1,0:T(8,128)(2,1)S(1)}, s32[64,1,128]{2,1,0:T(1,128)S(1)}) custom-call(s32[128]{0:T(128)S(1)} %bitcast.4, s32[128]{0:T(128)S(1)} %bitcast.5, bf16[128,32,128]{2,1,0:T(8,128)(2,1)S(1)} %bitcast.3), custom_call_target="tpu_custom_call" | custom-call | tf_op jit(solution)/shard_map/pallas_call | solution.py:54
  4.0 0.0 copy-done.2
  4.0 0.0 copy-start
  4.0 1.3 copy-done
  5.3 122.3 %shard_map.56 = f32[192,1536]{1,0:T(8,128)S(1)} custom-call(bf16[64,4,32,128]{3,2,1,0:T(8,128)(2,1)S(1)} %get-tuple-element.7.send_ref, s32[64,1,128]{2,1,0:T(1,128)S(1)} %get-tuple-element.8.slots_ref, f32[192,1536]{1,0:T(8,128)S(1)} %copy-done, bf16[512,512]{1,0:T(8,128)(2,1)S(1)} %copy-done.2), custom_call_target="tpu_custom_call" | custom-call | tf_op jit(solution)/shard_map/pallas_call | solution.py:495
  127.6 1.0 copy.7
Async XLA Ops:
  0.0 1.2 copy-start.1
  1.2 0.7 copy-start.3
  1.9 0.7 copy-start.4
  2.5 1.5 %copy-start.2 = (bf16[512,512]{1,0:T(8,128)(2,1)S(1)}, bf16[512,512]{1,0:T(8,128)(2,1)}, u32[]{:S(2)}) copy-start(bf16[512,512]{1,0:T(8,128)(2,1)} %diag_ref.1) | copy-start | bytes 1572868
  4.0 1.3 copy-start
